TPU v7x, 32 devices: a whole 2x2x4 slice. The times are simulated.
32 devices in a mesh: grp: 4 (over x, core), dev: 8 (over z, y).
Axes of the slice: x: 2, y: 2, z: 4, core: 2. Of those that a mesh axis runs over, the one named last changes fastest.
Arguments:
- queries: bfloat16 [8192, 768], P(('grp', 'dev')), may hold values from -1.796875 to 1.796875
- query_slots: int32 [8192], P('grp'), may hold values from 0 to 2047, as said below
- w_res: bfloat16 [768, 768], replicated, may hold values from -0.21875 to 0.21875
- labels: bfloat16 [640, 128, 768], P(('grp', 'dev')), may hold values from -0.71875 to 0.71875
- blocks: int32 [64, 12], P('grp'), may hold values from 0 to 639, as said below
- positives: int32 [8192, 4], P(('grp', 'dev')), may hold values from 0 to 81919, as said below
Outputs:
- query_loss: float32 [8192], P(('grp', 'dev'))
- query_grad: bfloat16 [8192, 768], P(('grp', 'dev'))
- label_grad: bfloat16 [640, 128, 768], P(('grp', 'dev'))
- residual_grad: bfloat16 [768, 768], replicated
Inputs may be any that keep to these rules, and one draw needn't show every extreme that they name: `query_slots`: the rows of one grp index (rows g * 256 * 8 onward) hold a permutation of 0 to 2047; a place // 256 is the dev index that owns the query's cluster, and the 256 rows of every device send exactly 32 queries to each owner. Row c lists 12 different blocks, all held by devices of the same grp index as the cluster's owner (device c // 2). The 2 clusters of one device list at most 16 distinct blocks, of which at most 2 are held by any one device; for every device's clusters some holder reaches 2. `positives`: the 4 labels of row r are different and lie in 4 different blocks listed for cluster r // 128.
All inputs are finite; a program needn't handle non-finite values.
Results may differ from a plain program's by a relative error of at most 0.0047.
The roundings to bfloat16 on the way count: a program that leaves them out, or rounds other values in their place, can miss the bound.
Values may be sent and summed in bfloat16 or wider, within the bound.
A program may use at most 128 MiB of HBM per device.

v0:
```python
from functools import partial

import jax
import jax.numpy as jnp
from jax import lax
from jax.sharding import PartitionSpec as P

BLK = 128
CSIZE = 128
SHORT = 12
NPOS = 4
POOL = 16
BLK_DEV = 20


def activate(values):
    return jax.nn.gelu(values, approximate=True)


def activate_slope(values):
    return jax.vjp(activate, values)[1](jnp.ones_like(values))[0]


def request_plan(listed, owner_base, peer_count, per_owner):
    owners = listed // BLK_DEV - owner_base
    within = listed % BLK_DEV
    positions = jnp.arange(listed.shape[0], dtype=jnp.int32)
    earlier = positions[None, :] < positions[:, None]
    same_block = listed[:, None] == listed[None, :]
    leading = jnp.logical_not(jnp.any(same_block & earlier, axis=1))
    first_seen = jnp.argmax(same_block, axis=1)
    same_owner = owners[:, None] == owners[None, :]
    ranking = jnp.sum(same_owner & earlier & leading[None, :], axis=1)
    own_place = owners * per_owner + ranking
    placed = own_place[first_seen]
    target = jnp.where(leading, own_place, peer_count * per_owner)
    request_table = (
        jnp.full((peer_count * per_owner,), -1, jnp.int32).at[target].set(within, mode="drop")
    )
    return (placed, request_table.reshape(peer_count, per_owner))


def local(queries, query_slots, w_res, labels, blocks, positives):
    peer_count = lax.axis_size("dev")
    groups = lax.axis_size("grp")
    own_index = lax.axis_index("dev")
    group_index = lax.axis_index("grp")
    rows_dev = queries.shape[0]
    feature_width = queries.shape[1]
    per_peer = rows_dev // peer_count
    clusters_dev = rows_dev // CSIZE
    per_owner = (POOL + peer_count - 1) // peer_count
    slots_total = peer_count * per_owner
    own_slots = lax.dynamic_slice_in_dim(query_slots, own_index * rows_dev, rows_dev)
    outbound = jnp.argsort(own_slots // rows_dev, stable=True)
    slot_grid = query_slots.reshape(peer_count, rows_dev)
    grid_order = jnp.argsort(slot_grid // rows_dev, axis=1, stable=True)
    grid_sorted = jnp.take_along_axis(slot_grid, grid_order, axis=1)
    incoming = (
        lax.dynamic_slice_in_dim(grid_sorted, own_index * per_peer, per_peer, 1).reshape(rows_dev)
        - own_index * rows_dev
    )
    arrange = jnp.argsort(incoming)
    pre_act = jnp.dot(queries, w_res, preferred_element_type=jnp.float32)
    payload = (queries.astype(jnp.float32) + activate(pre_act)).astype(jnp.bfloat16)
    arrived = lax.all_to_all(
        payload[outbound].reshape(peer_count, per_peer, feature_width),
        "dev",
        split_axis=0,
        concat_axis=0,
        tiled=True,
    )
    arrived = arrived.reshape(rows_dev, feature_width)[arrange]
    listed_all = blocks.reshape(peer_count, clusters_dev * SHORT)
    owner_base = group_index * peer_count
    planner = partial(
        request_plan, owner_base=owner_base, peer_count=peer_count, per_owner=per_owner
    )
    places_all, tables_all = jax.vmap(planner)(listed_all)
    own_places = places_all[own_index].reshape(clusters_dev, SHORT)
    wanted_flat = tables_all[:, own_index, :].reshape(-1)
    block_range = jnp.arange(labels.shape[0], dtype=jnp.int32)
    reply_pick = (wanted_flat[:, None] == block_range[None, :]).astype(jnp.bfloat16)
    reply_blocks = jnp.einsum(
        "sb,bjd->sjd", reply_pick, labels, preferred_element_type=jnp.float32
    ).astype(jnp.bfloat16)
    fetched = lax.all_to_all(
        reply_blocks.reshape(peer_count, per_owner, BLK, feature_width),
        "dev",
        split_axis=0,
        concat_axis=0,
        tiled=True,
    )
    fetched = fetched.reshape(slots_total, BLK, feature_width)
    listed_ids = listed_all[own_index].reshape(clusters_dev, SHORT)
    cluster_rows = arrived.reshape(clusters_dev, CSIZE, feature_width)
    wanted_pos = positives.reshape(clusters_dev, CSIZE, NPOS)
    offsets = jnp.arange(BLK, dtype=jnp.int32)
    slot_range = jnp.arange(slots_total, dtype=jnp.int32)
    place_pick = (own_places[:, :, None] == slot_range[None, None, :]).astype(jnp.bfloat16)

    def per_cluster(running, pieces):
        rows_here, pick_here, ids_here, pos_here = pieces
        chosen = jnp.einsum(
            "ks,sjd->kjd", pick_here, fetched, preferred_element_type=jnp.float32
        ).astype(jnp.bfloat16)
        logits = jnp.einsum("qd,kjd->qkj", rows_here, chosen, preferred_element_type=jnp.float32)
        label_ids = ids_here[:, None] * BLK + offsets[None, :]
        targets = jnp.any(
            label_ids[None, :, :, None] == pos_here[:, None, None, :], axis=-1
        ).astype(jnp.float32)
        loss_rows = jnp.mean(jax.nn.softplus(logits) - targets * logits, axis=(1, 2))
        errors = (jax.nn.sigmoid(logits) - targets).astype(jnp.bfloat16)
        grad_rows = jnp.einsum(
            "qkj,kjd->qd", errors, chosen, preferred_element_type=jnp.float32
        ).astype(jnp.bfloat16)
        terms_cluster = jnp.einsum(
            "qkj,qd->kjd", errors, rows_here, preferred_element_type=jnp.float32
        )
        return (running, (loss_rows, grad_rows, terms_cluster))

    pieces = (cluster_rows, place_pick, listed_ids, wanted_pos)
    running, (losses, grads, terms) = lax.scan(per_cluster, jnp.zeros((), jnp.float32), pieces)
    selector = (own_places.reshape(-1)[:, None] == slot_range[None, :]).astype(jnp.float32)
    summed = jnp.einsum(
        "rs,rjd->sjd",
        selector,
        terms.reshape(-1, BLK, feature_width),
        precision=lax.Precision.HIGHEST,
        preferred_element_type=jnp.float32,
    )
    returned_grads = lax.all_to_all(
        summed.astype(jnp.bfloat16).reshape(peer_count, per_owner, BLK, feature_width),
        "dev",
        split_axis=0,
        concat_axis=0,
        tiled=True,
    )
    returned_grads = returned_grads.reshape(slots_total, BLK, feature_width)
    label_grad = jnp.einsum(
        "sb,sjd->bjd", reply_pick, returned_grads, preferred_element_type=jnp.float32
    ).astype(jnp.bfloat16)
    cluster_grad = grads.reshape(rows_dev, feature_width)
    returned = lax.all_to_all(
        cluster_grad[incoming].reshape(peer_count, per_peer, feature_width),
        "dev",
        split_axis=0,
        concat_axis=0,
        tiled=True,
    )
    restored = returned.reshape(rows_dev, feature_width)[jnp.argsort(outbound)]
    grad_pre = (restored.astype(jnp.float32) * activate_slope(pre_act)).astype(jnp.bfloat16)
    back_term = jnp.einsum("qe,de->qd", grad_pre, w_res, preferred_element_type=jnp.float32)
    query_grad = (restored.astype(jnp.float32) + back_term).astype(jnp.bfloat16)
    weight_term = jnp.einsum("qd,qe->de", queries, grad_pre, preferred_element_type=jnp.float32)
    weight_sum = lax.psum(weight_term, ("grp", "dev"))
    scale_factor = float(rows_dev * peer_count * groups) ** (-0.5)
    return (
        losses.reshape(rows_dev),
        query_grad,
        label_grad,
        (weight_sum * scale_factor).astype(jnp.bfloat16),
    )


def solution(mesh):
    in_specs = (
        P(("grp", "dev"), None),
        P("grp"),
        P(),
        P(("grp", "dev"), None, None),
        P("grp", None),
        P(("grp", "dev"), None),
    )
    out_specs = (P(("grp", "dev")), P(("grp", "dev"), None), P(("grp", "dev"), None, None), P())
    return jax.shard_map(local, mesh=mesh, in_specs=in_specs, out_specs=out_specs, check_vma=False)
```

profile of v0, /device:TPU:0, one launch (start us, length us, event | category | flops | bytes accessed | tf_op | source)
XLA Modules:
  0.0 409.8 jit_solution(16528587998550061506)
XLA Ops:
  7.2 0.9 and_select_fusion
  8.1 3.2 sort.65
  11.3 2.5 add_convert_fusion
  13.8 1.9 gather_fusion
  15.7 7.3 %all-to-all-start = ((bf16[8,32,768]{2,1,0:T(8,128)(2,1)}), bf16[8,32,768]{2,1,0:T(8,128)(2,1)S(1)}, u32[]{:S(2)}, u32[]{:S(2)}) async-start(bf16[8,32,768]{2,1,0:T(8,128)(2,1)} %bitcast), calls=%async_computation | async-start | bytes 786432 | tf_op jit(solution)/shard_map/all_to_all | solution.py:66
  24.1 9.3 %scatter_fusion = s32[8,16]{1,0:T(8,128)S(1)} fusion(s32[8,16]{1,0:T(8,128)S(1)} %broadcast_in_dim.65, s32[192]{0:T(256)S(1)} %reshape.329, s32[192]{0:T(256)S(1)} %reshape.331), kind=kCustom, calls=%fused_computation.6 | custom fusion | bytes 3840 | tf_op jit(solution)/shard_map/vmap()/scatter | solution.py:38
  33.6 6.7 %fusion.23 = bf16[16,128,768]{2,0,1:T(8,128)(2,1)} fusion(bf16[20,128,768]{2,1,0:T(8,128)(2,1)} %param.11, s32[16]{0:T(128)S(1)} %eq.100), kind=kOutput, calls=%fused_computation.43 | convolution fusion | flops 64487744 | bytes 7077952 | tf_op jit(solution)/shard_map/sb,bjd->sjd/dot_general | solution.py:84
  40.3 7.3 %reshape.275 = bf16[8,2,128,768]{3,1,0,2:T(2,128)(2,1)} reshape(bf16[16,128,768]{2,0,1:T(8,128)(2,1)} %fusion.23) | data formatting | bytes 6291456 | tf_op jit(solution)/shard_map/reshape | solution.py:88
  47.6 5.7 %copy.80 = bf16[8,2,128,768]{3,1,2,0:T(2,128)(2,1)} copy(bf16[8,2,128,768]{3,1,0,2:T(2,128)(2,1)} %reshape.275) | data formatting | bytes 6291456 | tf_op jit(solution)/shard_map/reshape | solution.py:88
  53.3 6.1 %all-to-all-start.1 = ((bf16[8,2,128,768]{3,1,2,0:T(2,128)(2,1)}), bf16[8,2,128,768]{3,1,2,0:T(2,128)(2,1)}, u32[]{:S(2)}, u32[]{:S(2)}) async-start(bf16[8,2,128,768]{3,1,2,0:T(2,128)(2,1)} %copy.80), calls=%async_computation.1 | async-start | bytes 6291456 | tf_op jit(solution)/shard_map/all_to_all | solution.py:87
  60.9 1.0 compare_reduce_fusion.1
  62.0 1.2 gather_fusion.5
  63.6 2.1 sort.70.cloned.1.call-done
  65.7 0.7 fusion.40
  66.4 13.0 %gather_fusion.4 = s32[2048]{0:T(1024)S(1)} fusion(s32[8,256]{1,0:T(8,128)S(1)} %reshape.270, s32[2048]{0:T(1024)S(1)} %bitcast.111), kind=kCustom, calls=%fused_computation.4 | custom fusion | bytes 32768 | tf_op jit(solution)/shard_map/jit(take_along_axis)/gather | solution.py:58
  79.7 3.2 sort.67
  82.9 1.2 gather_fusion.1
  84.1 45.6 %all-to-all-done.1 = bf16[8,2,128,768]{3,1,2,0:T(2,128)(2,1)} async-done(((bf16[8,2,128,768]{3,1,2,0:T(2,128)(2,1)}), bf16[8,2,128,768]{3,1,2,0:T(2,128)(2,1)}, u32[]{:S(2)}, u32[]{:S(2)}) %all-to-all-start.1) | async-done | bytes 3145760 | tf_op jit(solution)/shard_map/all_to_all | solution.py:87
  129.7 2.4 copy.81
  132.2 3.4 copy.82
  135.6 28.0 %while.15 = (s32[]{:T(128)}, f32[2,128]{1,0:T(2,128)S(1)}, bf16[2,128,768]{2,1,0:T(8,128)(2,1)S(1)}, f32[2,12,128,768]{3,2,1,0:T(8,128)}, bf16[2,128,768]{2,1,0:...) while((s32[]{:T(128)}, f32[2,128]{1,0:T(2,128)S(1)}, ...), condition=%wide.region_10.11_spmd.clone, body=%wide.region_7.10_spmd.clone.sunk | while | flops 950879744 | bytes 30172984 | solution.py:123
  136.4 2.8 fusion.88
  139.3 1.6 copy-done.1
  140.9 1.6 fusion.89
  143.1 3.5 fusion.90
  146.6 2.9 bitcast_dynamic-update-slice_fusion.2
  150.4 2.8 fusion.88
  153.3 1.6 copy-done.1
  154.9 1.6 fusion.89
  157.1 3.5 fusion.90
  160.6 2.9 bitcast_dynamic-update-slice_fusion.2
  163.6 1.9 gather_fusion.2
  165.5 3.9 all-to-all-start.2
  169.4 14.2 %fusion.26 = bf16[16,128,768]{2,0,1:T(8,128)(2,1)} fusion(f32[24,128,768]{2,1,0:T(8,128)} %bitcast.116, s32[24]{0:T(128)S(1)} %get-tuple-element.162), kind=kOutput, calls=%fused_computation.44 | convolution fusion | flops 454558080 | bytes 12583008 | tf_op jit(solution)/shard_map/rs,rjd->sjd/dot_general | solution.py:125
  183.6 7.5 %reshape.283 = bf16[8,2,128,768]{3,1,0,2:T(2,128)(2,1)} reshape(bf16[16,128,768]{2,0,1:T(8,128)(2,1)} %fusion.26) | data formatting | bytes 6291456 | tf_op jit(solution)/shard_map/reshape | solution.py:133
  191.1 5.7 %copy.84 = bf16[8,2,128,768]{3,1,2,0:T(2,128)(2,1)} copy(bf16[8,2,128,768]{3,1,0,2:T(2,128)(2,1)} %reshape.283) | data formatting | bytes 6291456 | tf_op jit(solution)/shard_map/reshape | solution.py:133
  196.8 6.0 %all-to-all-start.3 = ((bf16[8,2,128,768]{3,1,2,0:T(2,128)(2,1)}), bf16[8,2,128,768]{3,1,2,0:T(2,128)(2,1)}, u32[]{:S(2)}, u32[]{:S(2)}) async-start(bf16[8,2,128,768]{3,1,2,0:T(2,128)(2,1)} %copy.84), calls=%async_computation.3 | async-start | bytes 6291456 | tf_op jit(solution)/shard_map/all_to_all | solution.py:132
  202.9 3.2 sort.68
  206.1 1.2 gather_fusion.3
  207.3 2.4 convolution_bitcast_fusion.1
  209.7 1.6 fusion.29
  211.3 168.4 %all-reduce.2.cloned.1.call-done = f32[768,768]{0,1:T(8,128)} async-done(((f32[768,768]{0,1:T(8,128)}), f32[768,768]{0,1:T(8,128)}) %all-reduce.2.cloned.1.call-update) | async-done | bytes 2359312 | tf_op jit(solution)/shard_map/psum | solution.py:156
  379.8 1.9 multiply_convert_fusion
  381.7 1.5 copy.87
  383.1 5.7 %copy.85 = bf16[8,2,128,768]{3,1,0,2:T(2,128)(2,1)} copy(bf16[8,2,128,768]{3,1,2,0:T(2,128)(2,1)} %all-to-all-done.3) | data formatting | bytes 6291456 | tf_op jit(solution)/shard_map/all_to_all | solution.py:132
  388.8 7.6 %reshape.284 = bf16[16,128,768]{2,0,1:T(8,128)(2,1)} reshape(bf16[8,2,128,768]{3,1,0,2:T(2,128)(2,1)} %copy.85) | data formatting | bytes 6291456 | tf_op jit(solution)/shard_map/reshape | solution.py:139
  396.4 3.4 convolution_convert_fusion
  399.8 2.8 copy.86
  (91 shorter events, 6.6 us)
Async XLA Ops:
  7.2 4.1 copy-start
  11.2 11.8 %copy-start.2 = (s32[16,12]{1,0:T(8,128)S(1)}, s32[16,12]{1,0:T(8,128)}, u32[]{:S(2)}) copy-start(s32[16,12]{1,0:T(8,128)} %param.12) | copy-start | bytes 2308
  15.7 37.6 %all-to-all-start = ((bf16[8,32,768]{2,1,0:T(8,128)(2,1)}), bf16[8,32,768]{2,1,0:T(8,128)(2,1)S(1)}, u32[]{:S(2)}, u32[]{:S(2)}) async-start(bf16[8,32,768]{2,1,0:T(8,128)(2,1)} %bitcast), calls=%async_computation | async-start | bytes 786432 | tf_op jit(solution)/shard_map/all_to_all | solution.py:66
  53.3 6.4 %copy-start.5 = (s32[2048]{0:T(1024)S(1)}, s32[2048]{0:T(1024)}, u32[]{:S(2)}) copy-start(s32[2048]{0:T(1024)} %param.9) | copy-start | bytes 24580
  53.3 76.4 %all-to-all-start.1 = ((bf16[8,2,128,768]{3,1,2,0:T(2,128)(2,1)}), bf16[8,2,128,768]{3,1,2,0:T(2,128)(2,1)}, u32[]{:S(2)}, u32[]{:S(2)}) async-start(bf16[8,2,128,768]{3,1,2,0:T(2,128)(2,1)} %copy.80), calls=%async_computation.1 | async-start | bytes 6291456 | tf_op jit(solution)/shard_map/all_to_all | solution.py:87
  59.5 6.3 %sort.70.cloned.1.call-start = ((), (), s32[]{:S(2)}) async-start(), calls=%async_computation.5 | async-start | bytes 49184 | tf_op jit(solution)/shard_map/jit(argsort)/sort | solution.py:57
  66.4 13.0 %copy-start.3 = (s32[8,256]{1,0:T(8,128)S(1)}, s32[8,256]{1,0:T(8,128)}, u32[]{:S(2)}) copy-start(s32[8,256]{1,0:T(8,128)} %get-tuple-element.64) | copy-start | bytes 24580
  132.1 3.4 copy-start.4
  139.3 1.6 copy-start.1
  153.3 1.6 copy-start.1
  163.6 20.0 %copy-start.7 = (f32[2,128]{1,0:T(2,128)}, f32[2,128]{1,0:T(2,128)S(1)}, u32[]{:S(2)}) copy-start(f32[2,128]{1,0:T(2,128)S(1)} %get-tuple-element.67) | copy-start | bytes 3076
  165.5 31.3 %all-to-all-start.2 = ((bf16[8,32,768]{2,1,0:T(8,128)(2,1)}), bf16[8,32,768]{2,1,0:T(8,128)(2,1)S(1)}, u32[]{:S(2)}, u32[]{:S(2)}) async-start(bf16[8,32,768]{2,1,0:T(8,128)(2,1)} %bitcast.14), calls=%async_computation.2 | async-start | bytes 786432 | tf_op jit(solution)/shard_map/all_to_all | solution.py:144
  196.8 186.3 %all-to-all-start.3 = ((bf16[8,2,128,768]{3,1,2,0:T(2,128)(2,1)}), bf16[8,2,128,768]{3,1,2,0:T(2,128)(2,1)}, u32[]{:S(2)}, u32[]{:S(2)}) async-start(bf16[8,2,128,768]{3,1,2,0:T(2,128)(2,1)} %copy.84), calls=%async_computation.3 | async-start | bytes 6291456 | tf_op jit(solution)/shard_map/all_to_all | solution.py:132
  202.8 4.4 %copy-start.6 = (bf16[256,768]{1,0:T(8,128)(2,1)S(1)}, bf16[256,768]{1,0:T(8,128)(2,1)}, u32[]{:S(2)}) copy-start(bf16[256,768]{1,0:T(8,128)(2,1)} %param.8) | copy-start | bytes 1179652
  202.8 4.5 %copy-start.8 = (f32[256,768]{1,0:T(8,128)S(1)}, f32[256,768]{1,0:T(8,128)}, u32[]{:S(2)}) copy-start(f32[256,768]{1,0:T(8,128)} %get-tuple-element.167) | copy-start | bytes 2359300
  202.8 176.9 %all-reduce.2.cloned.1.call-start = ((), (), s32[]{:S(2)}) async-start(), calls=%async_computation.4 | async-start | bytes 4718592 | tf_op jit(solution)/shard_map/psum | solution.py:156
Sparse Core Ops, SparseCore 0:
  63.2 2.2 sort.72.cloned.1.call-done
  210.2 169.5 all-reduce.1
  (1 shorter events, 0.0 us)
where the time goes:
time: 418 us; the launch traced here: 410 us
  waiting for transfers between devices  214 us (51%)
  local copies, waits for them, and re-layouts  87.3 us (21%)
  matrix products  52.5 us (13%)
  starting transfers between devices  23.3 us (6%)
  other arithmetic  17.8 us (4%)
  between operations  14.7 us (4%)
    psum x1, waiting for transfers between devices, local(): weight_sum = lax.psum(weight_term, ('grp', 'dev'))  168 us
    all_to_all x1, waiting for transfers between devices, local(): lax.all_to_all(reply_blocks.reshape(peer_count, per_owner, BLK, feature_w...  45.6 us
    dot_general x1, matrix products, local(): jnp.einsum('rs,rjd->sjd', selector, terms.reshape(-1, BLK, feature_width)...  14.2 us
    reshape x2, local copies, waits for them, and re-layouts, local(): summed.astype(jnp.bfloat16)  13.2 us
    gather x2, local copies, waits for them, and re-layouts, local(): grid_sorted = jnp.take_along_axis(slot_grid, grid_order, axis=1)  13 us
    reshape x2, local copies, waits for them, and re-layouts, local(): reply_blocks.reshape(peer_count, per_owner, BLK, feature_width)  13 us
    scatter x3, local copies, waits for them, and re-layouts, request_plan(): jnp.full((peer_count * per_owner,), -1, jnp.int32).at[target]  9.44 us
  transfers between devices with their start and end apart: 5, of which 2 were waited for; matrix products, arithmetic and copies ran while one was open for 22% of the time, Pallas kernels for 0%

commit v1 on v0

v1 whole, which is shorter than its diff:
```python
import functools

import jax
import jax.numpy as jnp
from jax import lax
from jax.experimental import pallas as pl
from jax.experimental.pallas import tpu as pltpu
from jax.sharding import PartitionSpec as P

BLK = 128
CSIZE = 128
SHORT = 12
NPOS = 4
UNITS = 2
MESH = pl.DeviceIdType.MESH
F32 = jnp.float32
BF16 = jnp.bfloat16


def activate(values):
    return jax.nn.gelu(values, approximate=True)


def activate_slope(values):
    return jax.vjp(activate, values)[1](jnp.ones_like(values))[0]


def remote(src, dst, send, recv, where):
    return pltpu.make_async_remote_copy(
        src_ref=src, dst_ref=dst, send_sem=send, recv_sem=recv, device_id=where, device_id_type=MESH
    )


def greet(targets):
    barrier = pltpu.get_barrier_semaphore()
    for where in targets:
        pl.semaphore_signal(barrier, inc=1, device_id=where, device_id_type=MESH)
    pl.semaphore_wait(barrier, len(targets))


def dev_peers(peers):
    me = lax.axis_index("dev")
    return [{"dev": lax.rem(me + d, peers)} for d in range(1, peers)]


def gather_kernel(peers, hid, meta, hall, mall, own, zs, zr, ys, yr, ms, mr):
    me = lax.axis_index("dev")
    inner, outer, lines = lax.rem(me, 2), me // 2, peers // 2
    partner = {"dev": outer * 2 + 1 - inner}
    greet(dev_peers(peers))
    local_h = pltpu.make_async_copy(hid, hall.at[me], own.at[0])
    local_m = pltpu.make_async_copy(meta, mall.at[me], own.at[1])
    along, across, small = [], [], []
    across.append(remote(hid, hall.at[me], ys.at[0], yr.at[0], partner))
    for d in range(1, lines):
        there = {"dev": lax.rem(outer + d, lines) * 2 + inner}
        along.append(remote(hid, hall.at[me], zs.at[d], zr.at[d], there))
    for d in range(1, peers):
        there = {"dev": lax.rem(me + d, peers)}
        small.append(remote(meta, mall.at[me], ms.at[d], mr.at[d], there))
    for copy in along + across + small:
        copy.start()
    local_h.start()
    local_m.start()
    for d in range(1, lines):
        source = lax.rem(outer + lines - d, lines) * 2 + inner
        along[d - 1].wait_recv()
        copy = remote(hall.at[source], hall.at[source], ys.at[d], yr.at[d], partner)
        copy.start()
        across.append(copy)
    for copy in along:
        copy.wait_send()
    for copy in across + small:
        copy.wait()
    local_h.wait()
    local_m.wait()


def cluster_kernel(table, hall, meta, labels, grads, losses, label_grad, total):
    step = pl.program_id(0)
    peers, _, per, width = hall.shape
    rows = peers * per

    @pl.when(step == 0)
    def _():
        total[...] = jnp.zeros_like(total)

    data = hall[...].reshape(rows, width)
    member = meta[0, NPOS:NPOS + 1, :]
    lanes = lax.broadcasted_iota(jnp.int32, (BLK, rows), 0)
    grad = jnp.zeros((rows, width), F32)
    loss = jnp.zeros((1, rows), F32)
    for unit in range(UNITS):
        block = table[step, unit]
        base = table[step, 6] + block * BLK
        listed = jnp.where(member == 0, table[step, 2 + 2 * unit], table[step, 3 + 2 * unit])
        live = listed > 0
        vectors = labels[block]
        logits = lax.dot_general(
            vectors, data, (((1,), (1,)), ((), ())), preferred_element_type=F32
        )
        hit = lanes == meta[0, 0:1, :] - base
        for n in range(1, NPOS):
            hit = hit | (lanes == meta[0, n:n + 1, :] - base)
        small = jnp.exp(-jnp.abs(logits))
        soft = jnp.maximum(logits, 0.0) + jnp.log1p(small)
        loss = loss + jnp.where(
            live, jnp.sum(soft - jnp.where(hit, logits, 0.0), axis=0, keepdims=True), 0.0
        )
        chance = jnp.where(logits >= 0, 1.0, small) / (1.0 + small)
        wrong = jnp.where(live, chance - jnp.where(hit, 1.0, 0.0), 0.0).astype(BF16)
        grad = grad + lax.dot_general(
            wrong, vectors, (((0,), (0,)), ((), ())), preferred_element_type=F32
        )
        term = jnp.dot(wrong, data, preferred_element_type=F32)
        total[block] = total[block] + term.astype(BF16).astype(F32)
    grads[...] = grad.astype(BF16).reshape(grads.shape)
    losses[0] = jnp.broadcast_to(loss * (1.0 / (SHORT * BLK)), losses.shape[1:])

    @pl.when(step == pl.num_programs(0) - 1)
    def _():
        label_grad[...] = total[...].astype(BF16)


def scatter_kernel(peers, grads, losses, out, loss_out, yb, hb, zb, lb, ys, yr, zs, zr, ls, lr):
    me = lax.axis_index("dev")
    inner, outer, lines = lax.rem(me, 2), me // 2, peers // 2
    partner = {"dev": outer * 2 + 1 - inner}
    greet(dev_peers(peers))
    across, along, small = [], [], []
    for k in range(lines):
        line = lax.rem(outer + 1 + k, lines)
        across.append(remote(grads.at[line * 2 + 1 - inner], yb.at[k], ys.at[k], yr.at[k], partner))
    for d in range(1, peers):
        dest = lax.rem(me + d, peers)
        small.append(remote(losses.at[dest], lb.at[d], ls.at[d], lr.at[d], {"dev": dest}))
    for copy in across + small:
        copy.start()
    for k in range(lines):
        line = lax.rem(outer + 1 + k, lines)
        across[k].wait_recv()
        pair = grads[line * 2 + inner].astype(F32) + yb[k].astype(F32)
        hb[k] = pair.astype(BF16)
        if k < lines - 1:
            copy = remote(hb.at[k], zb.at[k], zs.at[k], zr.at[k], {"dev": line * 2 + inner})
            copy.start()
            along.append(copy)
    for copy in small:
        copy.wait()
    loss = losses[me]
    for d in range(1, peers):
        loss = loss + lb[d]
    loss_out[...] = loss
    for copy in along:
        copy.wait()
    acc = hb[lines - 1].astype(F32)
    for k in range(lines - 1):
        acc = acc + zb[k].astype(F32)
    out[...] = acc.astype(BF16)
    for copy in across:
        copy.wait_send()


def sum_kernel(peers, groups, scale, term, out, b1, t1, b2, t2, b3, sends, recvs):
    me, group = lax.axis_index("dev"), lax.axis_index("grp")
    core, chip, chips = lax.rem(group, 2), group // 2, groups // 2
    partner = {"grp": chip * 2 + 1 - core}
    chip_at = [lax.rem(chip + d, chips) for d in range(chips)]
    dev_at = [lax.rem(me + d, peers) for d in range(peers)]
    greet(
        [partner]
        + [{"grp": chip_at[d] * 2 + core} for d in range(1, chips)]
        + [{"dev": dev_at[d]} for d in range(1, peers)]
    )
    used = [0]

    def make(src, dst, where):
        at = used[0]
        used[0] += 1
        return remote(src, dst, sends.at[at], recvs.at[at], where)

    def run(copies):
        for copy in copies:
            copy.start()
        for copy in copies:
            copy.wait()

    run([make(term.at[1 - core], b1, partner)])
    t1[...] = (term[core].astype(F32) + b1[...].astype(F32)).astype(BF16)
    run([make(t1.at[chip_at[d]], b2.at[d], {"grp": chip_at[d] * 2 + core}) for d in range(1, chips)])
    acc = t1[chip].astype(F32)
    for d in range(1, chips):
        acc = acc + b2[d].astype(F32)
    t2[...] = acc.astype(BF16)
    run([make(t2.at[dev_at[d]], b3.at[d], {"dev": dev_at[d]}) for d in range(1, peers)])
    acc = t2[me].astype(F32)
    for d in range(1, peers):
        acc = acc + b3[d].astype(F32)
    out[core, chip, me] = (acc * scale).astype(BF16)
    mine = out.at[core, chip, me]
    run([make(mine, mine, {"dev": dev_at[d]}) for d in range(1, peers)])
    mine = out.at[core, chip]
    run([make(mine, mine, {"grp": chip_at[d] * 2 + core}) for d in range(1, chips)])
    run([make(out.at[core], out.at[core], partner)])


def params(collective=None):
    more = {} if collective is None else dict(collective_id=collective, has_side_effects=True)
    return pltpu.CompilerParams(vmem_limit_bytes=48 * 1024 * 1024, **more)


def local(queries, query_slots, w_res, labels, blocks, positives):
    peers = lax.axis_size("dev")
    groups = lax.axis_size("grp")
    me = lax.axis_index("dev")
    group = lax.axis_index("grp")
    rows, width = queries.shape
    held = labels.shape[0]
    per = rows // peers
    lines = peers // 2
    chips = groups // 2
    vmem = pl.BlockSpec(memory_space=pltpu.VMEM)
    anywhere = pl.BlockSpec(memory_space=pl.ANY)
    dma = pltpu.SemaphoreType.DMA

    slot_grid = query_slots.reshape(peers, rows)
    slot_sorted = jnp.sort(slot_grid, axis=1)
    own_slots = lax.dynamic_index_in_dim(slot_grid, me, 0, keepdims=False)
    own_sorted = lax.dynamic_index_in_dim(slot_sorted, me, 0, keepdims=False)
    order = (own_sorted[:, None] == own_slots[None, :]).astype(BF16)
    place = lax.dynamic_slice_in_dim(slot_sorted, me * per, per, 1).reshape(rows) - me * rows
    arrange = place[None, :] == jnp.arange(rows, dtype=jnp.int32)[:, None]
    wanted = jnp.sum(jnp.where(arrange[None], positives.T[:, :, None], 0), axis=1)
    meta = jnp.concatenate(
        [wanted, (place // CSIZE)[None], jnp.zeros((8 - NPOS - 1, rows), jnp.int32)], axis=0
    )
    first = (group * peers + me) * held
    listed = blocks.reshape(peers, rows // CSIZE, SHORT) - first
    inside = (listed >= 0) & (listed < held)
    low = jnp.min(jnp.where(inside, listed, held), axis=(1, 2))
    high = jnp.max(jnp.where(inside, listed, -1), axis=(1, 2))
    flag_low = jnp.any(inside & (listed == low[:, None, None]), axis=2).astype(jnp.int32)
    flag_high = jnp.any(inside & (listed == high[:, None, None]), axis=2).astype(jnp.int32)
    flag_high = jnp.where((high > low)[:, None], flag_high, 0)
    table = jnp.concatenate(
        [
            jnp.minimum(low, held - 1)[:, None],
            jnp.maximum(high, 0)[:, None],
            flag_low,
            flag_high,
            jnp.broadcast_to(first * BLK, (peers, 1)),
        ],
        axis=1,
    )

    ordered = jnp.dot(order, queries, preferred_element_type=F32).astype(BF16)
    pre = jnp.dot(ordered, w_res, preferred_element_type=F32)
    hidden = (ordered.astype(F32) + activate(pre)).astype(BF16)

    hall, mall = pl.pallas_call(
        functools.partial(gather_kernel, peers),
        out_shape=(
            jax.ShapeDtypeStruct((peers, peers, per, width), BF16),
            jax.ShapeDtypeStruct((peers, 8, rows), jnp.int32),
        ),
        in_specs=[anywhere, anywhere],
        out_specs=(anywhere, anywhere),
        scratch_shapes=[
            dma((2,)), dma((lines,)), dma((lines,)), dma((lines,)), dma((lines,)),
            dma((peers,)), dma((peers,)),
        ],
        compiler_params=params(0),
    )(hidden.reshape(peers, per, width), meta)

    grads, losses, label_grad = pl.pallas_call(
        cluster_kernel,
        grid_spec=pltpu.PrefetchScalarGridSpec(
            num_scalar_prefetch=1,
            grid=(peers,),
            in_specs=[
                pl.BlockSpec((peers, 1, per, width), lambda p, t: (0, p, 0, 0)),
                pl.BlockSpec((1, 8, rows), lambda p, t: (p, 0, 0)),
                pl.BlockSpec((held, BLK, width), lambda p, t: (0, 0, 0)),
            ],
            out_specs=[
                pl.BlockSpec((peers, 1, per, width), lambda p, t: (0, p, 0, 0)),
                pl.BlockSpec((1, 8, rows), lambda p, t: (p, 0, 0)),
                pl.BlockSpec((held, BLK, width), lambda p, t: (0, 0, 0)),
            ],
            scratch_shapes=[pltpu.VMEM((held, BLK, width), F32)],
        ),
        out_shape=(
            jax.ShapeDtypeStruct((peers, peers, per, width), BF16),
            jax.ShapeDtypeStruct((peers, 8, rows), F32),
            jax.ShapeDtypeStruct(labels.shape, BF16),
        ),
        compiler_params=params(),
    )(table, hall, mall, labels)

    hidden_grad, loss_sum = pl.pallas_call(
        functools.partial(scatter_kernel, peers),
        out_shape=(
            jax.ShapeDtypeStruct((peers, per, width), BF16),
            jax.ShapeDtypeStruct((8, rows), F32),
        ),
        in_specs=[vmem, vmem],
        out_specs=(vmem, vmem),
        scratch_shapes=[
            pltpu.VMEM((lines, peers, per, width), BF16),
            pltpu.VMEM((lines, peers, per, width), BF16),
            pltpu.VMEM((lines, peers, per, width), BF16),
            pltpu.VMEM((peers, 8, rows), F32),
            dma((lines,)), dma((lines,)), dma((lines,)), dma((lines,)),
            dma((peers,)), dma((peers,)),
        ],
        compiler_params=params(1),
    )(grads, losses)
    hidden_grad = hidden_grad.reshape(rows, width).astype(F32)

    loss_rows = jnp.sum(jnp.where(arrange, loss_sum[0][None, :], 0.0), axis=1)
    grad_pre = (hidden_grad * activate_slope(pre)).astype(BF16)
    weight_term = lax.dot_general(
        ordered, grad_pre, (((0,), (0,)), ((), ())), preferred_element_type=F32
    )
    tall, wide = width // (2 * chips * lines), width // 2
    pieces = weight_term.astype(BF16).reshape(2, chips, lines, tall, 2, wide)
    pieces = pieces.transpose(0, 1, 4, 2, 3, 5).reshape(2, chips, peers, tall, wide)
    count = 2 + 2 * (chips - 1) + 2 * (peers - 1)
    summed = pl.pallas_call(
        functools.partial(
            sum_kernel, peers, groups, float(rows * peers * groups) ** (-0.5)
        ),
        out_shape=jax.ShapeDtypeStruct(pieces.shape, BF16),
        in_specs=[vmem],
        out_specs=vmem,
        scratch_shapes=[
            pltpu.VMEM((chips, peers, tall, wide), BF16),
            pltpu.VMEM((chips, peers, tall, wide), BF16),
            pltpu.VMEM((chips, peers, tall, wide), BF16),
            pltpu.VMEM((peers, tall, wide), BF16),
            pltpu.VMEM((peers, tall, wide), BF16),
            dma((count,)), dma((count,)),
        ],
        compiler_params=params(2),
    )(pieces)
    residual_grad = summed.reshape(2, chips, 2, lines, tall, wide)
    residual_grad = residual_grad.transpose(0, 1, 3, 4, 2, 5).reshape(width, width)

    back_term = jnp.einsum("qe,de->qd", grad_pre, w_res, preferred_element_type=F32)
    query_grad = (hidden_grad + back_term).astype(BF16)
    query_grad = lax.dot_general(
        order, query_grad, (((0,), (0,)), ((), ())), preferred_element_type=F32
    ).astype(BF16)
    return loss_rows, query_grad, label_grad, residual_grad


def solution(mesh):
    in_specs = (
        P(("grp", "dev"), None),
        P("grp"),
        P(),
        P(("grp", "dev"), None, None),
        P("grp", None),
        P(("grp", "dev"), None),
    )
    out_specs = (P(("grp", "dev")), P(("grp", "dev"), None), P(("grp", "dev"), None, None), P())
    return jax.shard_map(local, mesh=mesh, in_specs=in_specs, out_specs=out_specs, check_vma=False)
```

time: 418 us -> 194 us (0.46); the launches traced: 410 us -> 192 us
  waiting for transfers between devices: 214 us -> 0 us
  Pallas kernels: 0 us -> 159 us
  local copies, waits for them, and re-layouts: 87.3 us -> 9.88 us
  matrix products: 52.5 us -> 3.97 us
  starting transfers between devices: 23.3 us -> 0 us
  other arithmetic: 17.8 us -> 5.06 us
    psum x1 -> x0, waiting for transfers between devices: 168 us -> none  [local(): weight_sum = lax.psum(weight_term, ('grp', 'dev'))]
    pallas_call x0 -> x4, Pallas kernels: none -> 159 us  [the longest x1 52 us: local(): pl.pallas_call(functools.partial(scatter_kernel, peers), out_shape=(jax.S...]
    dot_general x14 -> x4, matrix products: 52.5 us -> 3.97 us  [the longest x1 1.54 us: local(): lax.dot_general(order, query_grad, (((0,), (0,)), ((), ())), preferred_el...]
    all_to_all x4 -> x0, waiting for transfers between devices: 45.6 us -> none  [the longest x1 45.6 us: local(): lax.all_to_all(reply_blocks.reshape(peer_count, per_owner, BLK, feature_w...]
    reshape x7 -> x3, local copies, waits for them, and re-layouts: 33.9 us -> 1.84 us  [the longest x1 1.38 us: local(): slot_grid = query_slots.reshape(peers, rows)]
    all_to_all x4 -> x0, starting transfers between devices: 23.3 us -> none  [the longest x1 7.28 us: local(): lax.all_to_all(payload[outbound].reshape(peer_count, per_peer, feature_wi...]
    gather x9 -> x0, local copies, waits for them, and re-layouts: 20.6 us -> none  [the longest x2 13 us: local(): grid_sorted = jnp.take_along_axis(slot_grid, grid_order, axis=1)]
    sort x3 -> x0, other arithmetic: 9.5 us -> none  [the longest x1 3.17 us: local(): arrange = jnp.argsort(incoming)]
  transfers between devices with their start and end apart: 5 -> 0, of which waited for: 2 -> 0; matrix products, arithmetic and copies ran while one was open for 22% -> 0% of each run, Pallas kernels for 0% -> 0%
where the time goes in v1:
time: 194 us; the launch traced here: 192 us
  Pallas kernels  159 us (82%)
  between operations  14.2 us (7%)
  local copies, waits for them, and re-layouts  9.88 us (5%)
  other arithmetic  5.06 us (3%)
  matrix products  3.97 us (2%)
    pallas_call x1, Pallas kernels, local(): pl.pallas_call(functools.partial(scatter_kernel, peers), out_shape=(jax.S...  52 us
    pallas_call x1, Pallas kernels, local(): pl.pallas_call(functools.partial(gather_kernel, peers), out_shape=(jax.Sh...  51.4 us
    pallas_call x1, Pallas kernels, local(): pl.pallas_call(functools.partial(sum_kernel, peers, groups, float(rows *...  37.3 us
    pallas_call x1, Pallas kernels, local(): pl.pallas_call(cluster_kernel, grid_spec=pltpu.PrefetchScalarGridSpec(num...  18 us

profile of v1, /device:TPU:0, one launch (start us, length us, event | category | flops | bytes accessed | tf_op | source)
XLA Modules:
  0.0 191.8 jit_solution(10332550242759991183)
XLA Ops:
  7.2 0.0 copy-start
  7.2 0.0 sort.10.cloned.1.call-start
  7.2 1.4 reshape.151
  8.6 0.0 sort.10.cloned.1.call-update
  8.6 0.8 select_reduce_fusion.2
  9.5 0.1 reduce_max.14
  9.5 0.1 reduce_max.18
  9.7 0.1 eq.67
  9.7 0.1 eq.68
  9.8 0.1 reduce_min.14
  9.9 0.1 reduce_min.18
  10.0 0.1 eq.63
  10.1 0.1 eq.64
  10.2 0.9 and_reduce_fusion
  11.1 0.1 reshape.158
  11.2 0.1 broadcast_select_fusion
  11.2 0.1 pad.2.clone
  11.3 0.1 copy.19
  11.4 0.1 reshape.157
  11.5 0.1 copy.18
  11.6 0.1 concatenate.6.table
  11.7 2.0 %sort.10.cloned.1.call-done = s32[8,256]{1,0:T(8,128)} async-done(((s32[8,256]{1,0:T(8,128)}), s32[8,256]{1,0:T(8,128)}) %sort.10.cloned.1.call-update) | async-done | bytes 8208 | tf_op jit(solution)/shard_map/jit(sort)/sort | solution.py:227
  13.7 0.8 dynamic-slice_subtract_fusion
  14.4 0.1 sub.43
  14.5 0.1 sub.46
  14.7 0.9 select_reduce_fusion
  15.6 0.7 constant_dynamic-slice_fusion
  16.3 1.3 convolution_convert_fusion.2
  17.6 0.0 copy-done
  17.6 0.6 add_convert_fusion
  18.2 0.1 add_add_fusion.meta
  18.3 51.4 %shard_map.93 = (bf16[8,8,32,768]{3,2,1,0:T(8,128)(2,1)S(1)}, s32[8,8,256]{2,1,0:T(8,128)S(1)}) custom-call(bf16[8,32,768]{2,1,0:T(8,128)(2,1)S(1)} %bitcast.30, s32[8,256]{1,0:T(8,128)S(1)} %add_add_fusion.meta), custom_call_target="tpu_custom_call" | custom-call | tf_op jit(solution)/shard_map/pallas_call | solution.py:260
  69.7 0.0 copy-start.1
  69.7 1.7 copy-done.1
  71.4 18.0 %shard_map.94 = (bf16[8,8,32,768]{3,2,1,0:T(8,128)(2,1)S(1)}, f32[8,8,256]{2,1,0:T(8,128)S(1)}, bf16[20,128,768]{2,1,0:T(8,128)(2,1)}) custom-call(s32[8,7]{1,0:T(8,128)S(1)} %concatenate.6.table, bf16[8,8,32,768]{3,2,1,0:T(8,128)(2,1)} %copy-done.1, s32[8,8,256]{2,1,0:T(8,128)S(1)} %get-tuple-element.12.meta, bf16[20,128,768]{2,1,0:T(8,128)(2,1)} %labels.1), custom_call_target="tpu_custom_call" | custom-call | tf_op jit(solution)/shard_map/pallas_call | solution.py:275
  89.4 52.0 %shard_map.95 = (bf16[8,32,768]{2,1,0:T(8,128)(2,1)S(1)}, f32[8,256]{1,0:T(8,128)S(1)}) custom-call(bf16[8,8,32,768]{3,2,1,0:T(8,128)(2,1)S(1)} %get-tuple-element.13.grads, f32[8,8,256]{2,1,0:T(8,128)S(1)} %get-tuple-element.14.losses), custom_call_target="tpu_custom_call" | custom-call | tf_op jit(solution)/shard_map/pallas_call | solution.py:300
  141.4 0.7 select_reduce_fusion.1
  142.1 0.6 fusion.2
  142.6 0.5 convolution_convert_fusion
  143.2 1.5 convolution_convert_fusion.1
  144.7 0.3 reshape.153
  145.0 0.2 copy.20
  145.2 37.3 %shard_map.96 = bf16[2,2,8,48,384]{4,3,2,1,0:T(8,128)(2,1)S(1)} custom-call(bf16[2,2,8,48,384]{4,3,2,1,0:T(8,128)(2,1)S(1)} %bitcast.28), custom_call_target="tpu_custom_call" | custom-call | tf_op jit(solution)/shard_map/pallas_call | solution.py:329
  182.5 1.2 copy.21
  183.7 1.2 copy.22
  (10 shorter events, 0.1 us)
Async XLA Ops:
  7.2 10.4 %copy-start = (bf16[768,768]{1,0:T(8,128)(2,1)S(1)}, bf16[768,768]{1,0:T(8,128)(2,1)}, u32[]{:S(2)}) copy-start(bf16[768,768]{1,0:T(8,128)(2,1)} %param.8) | copy-start | bytes 3538948
  7.2 6.5 %sort.10.cloned.1.call-start = ((), (), s32[]{:S(2)}) async-start(), calls=%async_computation | async-start | bytes 24608 | tf_op jit(solution)/shard_map/jit(sort)/sort | solution.py:227
  69.7 1.7 copy-start.1
Sparse Core Ops, SparseCore 0:
  10.9 2.5 sort.12.cloned.1.call-done
  (1 shorter events, 0.0 us)

commit v2 on v1

--- a/solution.py
+++ b/solution.py
@@ -43,34 +43,82 @@
     return [{"dev": lax.rem(me + d, peers)} for d in range(1, peers)]
 
 
-def gather_kernel(peers, hid, meta, hall, mall, own, zs, zr, ys, yr, ms, mr):
+def gather_kernel(peers, hid, meta, hall, mall, own, us, ur, ds, dr, ys, yr, ms, mr):
     me = lax.axis_index("dev")
     inner, outer, lines = lax.rem(me, 2), me // 2, peers // 2
+    top = lines - 1
     partner = {"dev": outer * 2 + 1 - inner}
+    above, below = {"dev": me + 2}, {"dev": me - 2}
     greet(dev_peers(peers))
+
+    def up(k, held=None):
+        spot = hall.at[me - 2 * k]
+        return remote(spot if held is None else held, spot, us.at[k], ur.at[k], above)
+
+    def down(k, held=None):
+        spot = hall.at[me + 2 * k]
+        return remote(spot if held is None else held, spot, ds.at[k], dr.at[k], below)
+
+    def across(line, held=None):
+        spot = hall.at[line * 2 + inner]
+        return remote(spot if held is None else held, spot, ys.at[line], yr.at[line], partner)
+
+    @pl.when(outer < top)
+    def _():
+        up(0, hid).start()
+
+    @pl.when(outer > 0)
+    def _():
+        down(0, hid).start()
+
+    across(outer, hid).start()
     local_h = pltpu.make_async_copy(hid, hall.at[me], own.at[0])
     local_m = pltpu.make_async_copy(meta, mall.at[me], own.at[1])
-    along, across, small = [], [], []
-    across.append(remote(hid, hall.at[me], ys.at[0], yr.at[0], partner))
-    for d in range(1, lines):
-        there = {"dev": lax.rem(outer + d, lines) * 2 + inner}
-        along.append(remote(hid, hall.at[me], zs.at[d], zr.at[d], there))
+    local_h.start()
+    local_m.start()
+    small = []
     for d in range(1, peers):
         there = {"dev": lax.rem(me + d, peers)}
         small.append(remote(meta, mall.at[me], ms.at[d], mr.at[d], there))
-    for copy in along + across + small:
+    for copy in small:
         copy.start()
-    local_h.start()
-    local_m.start()
-    for d in range(1, lines):
-        source = lax.rem(outer + lines - d, lines) * 2 + inner
-        along[d - 1].wait_recv()
-        copy = remote(hall.at[source], hall.at[source], ys.at[d], yr.at[d], partner)
-        copy.start()
-        across.append(copy)
-    for copy in along:
-        copy.wait_send()
-    for copy in across + small:
+    for k in range(lines - 1):
+
+        @pl.when(outer >= k + 1)
+        def _():
+            spot = hall.at[me - 2 * (k + 1)]
+            remote(spot, spot, us.at[k], ur.at[k], below).wait_recv()
+
+            @pl.when(outer < top)
+            def _():
+                up(k + 1).start()
+
+            across(outer - 1 - k).start()
+
+        @pl.when(outer + k + 1 <= top)
+        def _():
+            spot = hall.at[me + 2 * (k + 1)]
+            remote(spot, spot, ds.at[k], dr.at[k], above).wait_recv()
+
+            @pl.when(outer > 0)
+            def _():
+                down(k + 1).start()
+
+            across(outer + 1 + k).start()
+
+    for k in range(lines):
+
+        @pl.when((outer >= k) & (outer < top))
+        def _():
+            up(k).wait_send()
+
+        @pl.when((outer + k <= top) & (outer > 0))
+        def _():
+            down(k).wait_send()
+
+    for line in range(lines):
+        across(line).wait()
+    for copy in small:
         copy.wait()
     local_h.wait()
     local_m.wait()
@@ -78,86 +126,121 @@
 
 def cluster_kernel(table, hall, meta, labels, grads, losses, label_grad, total):
     step = pl.program_id(0)
-    peers, _, per, width = hall.shape
+    peers, owners, per, width = hall.shape
     rows = peers * per
 
     @pl.when(step == 0)
     def _():
         total[...] = jnp.zeros_like(total)
 
-    data = hall[...].reshape(rows, width)
-    member = meta[0, NPOS:NPOS + 1, :]
     lanes = lax.broadcasted_iota(jnp.int32, (BLK, rows), 0)
-    grad = jnp.zeros((rows, width), F32)
-    loss = jnp.zeros((1, rows), F32)
-    for unit in range(UNITS):
-        block = table[step, unit]
-        base = table[step, 6] + block * BLK
-        listed = jnp.where(member == 0, table[step, 2 + 2 * unit], table[step, 3 + 2 * unit])
-        live = listed > 0
-        vectors = labels[block]
+    for owner in range(owners):
+        at = step * owners + owner
+        data = hall[:, owner].reshape(rows, width)
+        member = meta[owner, NPOS:NPOS + 1, :]
+        vectors = jnp.concatenate([labels[table[at, unit]] for unit in range(UNITS)], axis=0)
         logits = lax.dot_general(
             vectors, data, (((1,), (1,)), ((), ())), preferred_element_type=F32
         )
-        hit = lanes == meta[0, 0:1, :] - base
-        for n in range(1, NPOS):
-            hit = hit | (lanes == meta[0, n:n + 1, :] - base)
         small = jnp.exp(-jnp.abs(logits))
         soft = jnp.maximum(logits, 0.0) + jnp.log1p(small)
-        loss = loss + jnp.where(
-            live, jnp.sum(soft - jnp.where(hit, logits, 0.0), axis=0, keepdims=True), 0.0
-        )
         chance = jnp.where(logits >= 0, 1.0, small) / (1.0 + small)
-        wrong = jnp.where(live, chance - jnp.where(hit, 1.0, 0.0), 0.0).astype(BF16)
-        grad = grad + lax.dot_general(
+        loss = jnp.zeros((1, rows), F32)
+        parts = []
+        for unit in range(UNITS):
+            base = table[at, 6] + table[at, unit] * BLK
+            listed = jnp.where(member == 0, table[at, 2 + 2 * unit], table[at, 3 + 2 * unit])
+            live = listed > 0
+            span = slice(unit * BLK, (unit + 1) * BLK)
+            hit = lanes == meta[owner, 0:1, :] - base
+            for n in range(1, NPOS):
+                hit = hit | (lanes == meta[owner, n:n + 1, :] - base)
+            gap = soft[span] - jnp.where(hit, logits[span], 0.0)
+            loss = loss + jnp.where(live, jnp.sum(gap, axis=0, keepdims=True), 0.0)
+            parts.append(jnp.where(live, chance[span] - jnp.where(hit, 1.0, 0.0), 0.0))
+        wrong = jnp.concatenate(parts, axis=0).astype(BF16)
+        grad = lax.dot_general(
             wrong, vectors, (((0,), (0,)), ((), ())), preferred_element_type=F32
         )
-        term = jnp.dot(wrong, data, preferred_element_type=F32)
-        total[block] = total[block] + term.astype(BF16).astype(F32)
-    grads[...] = grad.astype(BF16).reshape(grads.shape)
-    losses[0] = jnp.broadcast_to(loss * (1.0 / (SHORT * BLK)), losses.shape[1:])
+        term = jnp.dot(wrong, data, preferred_element_type=F32).astype(BF16).astype(F32)
+        for unit in range(UNITS):
+            block = table[at, unit]
+            total[block] = total[block] + term[unit * BLK:(unit + 1) * BLK]
+        grads[:, owner] = grad.astype(BF16).reshape(peers, per, width)
+        losses[owner] = jnp.broadcast_to(loss * (1.0 / (SHORT * BLK)), losses.shape[1:])
 
     @pl.when(step == pl.num_programs(0) - 1)
     def _():
         label_grad[...] = total[...].astype(BF16)
 
 
-def scatter_kernel(peers, grads, losses, out, loss_out, yb, hb, zb, lb, ys, yr, zs, zr, ls, lr):
+def scatter_kernel(
+    peers, grads, losses, out, loss_out, yb, hb, rb, acc, lb, ys, yr, zs, zr, ls, lr
+):
     me = lax.axis_index("dev")
     inner, outer, lines = lax.rem(me, 2), me // 2, peers // 2
+    top = lines - 1
     partner = {"dev": outer * 2 + 1 - inner}
+    orders = [sorted(range(lines), key=lambda at: -abs(at - o)) for o in range(lines)]
     greet(dev_peers(peers))
+
+    def pick(k):
+        line = orders[0][k]
+        for o in range(1, lines):
+            line = jnp.where(outer == o, orders[o][k], line)
+        return line
+
+    picked = [pick(k) for k in range(lines - 1)] + [outer]
     across, along, small = [], [], []
-    for k in range(lines):
-        line = lax.rem(outer + 1 + k, lines)
+    for k, line in enumerate(picked):
         across.append(remote(grads.at[line * 2 + 1 - inner], yb.at[k], ys.at[k], yr.at[k], partner))
     for d in range(1, peers):
         dest = lax.rem(me + d, peers)
         small.append(remote(losses.at[dest], lb.at[d], ls.at[d], lr.at[d], {"dev": dest}))
     for copy in across + small:
         copy.start()
-    for k in range(lines):
-        line = lax.rem(outer + 1 + k, lines)
+
+    def pair(k):
+        return grads[picked[k] * 2 + inner].astype(F32) + yb[k].astype(F32)
+
+    for k in range(lines - 1):
+        line = picked[k]
+        way = jnp.where(line > outer, 0, 1)
+        ahead = me + 2 - 4 * way
+        feeds = jnp.where(line > outer, outer, top - outer)
+        copy = remote(hb.at[k], rb.at[way, line], zs.at[k], zr.at[way, line], {"dev": ahead})
         across[k].wait_recv()
-        pair = grads[line * 2 + inner].astype(F32) + yb[k].astype(F32)
-        hb[k] = pair.astype(BF16)
-        if k < lines - 1:
-            copy = remote(hb.at[k], zb.at[k], zs.at[k], zr.at[k], {"dev": line * 2 + inner})
-            copy.start()
-            along.append(copy)
+
+        @pl.when(feeds == 0)
+        def _():
+            hb[k] = pair(k).astype(BF16)
+
+        @pl.when(feeds > 0)
+        def _():
+            copy.wait_recv()
+            hb[k] = (pair(k) + rb[way, line].astype(F32)).astype(BF16)
+
+        copy.start()
+        along.append(copy)
     for copy in small:
         copy.wait()
     loss = losses[me]
     for d in range(1, peers):
         loss = loss + lb[d]
     loss_out[...] = loss
-    for copy in along:
-        copy.wait()
-    acc = hb[lines - 1].astype(F32)
-    for k in range(lines - 1):
-        acc = acc + zb[k].astype(F32)
-    out[...] = acc.astype(BF16)
-    for copy in across:
+    across[top].wait_recv()
+    acc[...] = pair(top)
+    for way, present in enumerate((outer > 0, outer < top)):
+
+        @pl.when(present)
+        def _():
+            spot = rb.at[way, outer]
+            near = {"dev": me - 2 + 4 * way}
+            remote(spot, spot, zs.at[0], zr.at[way, outer], near).wait_recv()
+            acc[...] += rb[way, outer].astype(F32)
+
+    out[...] = acc[...].astype(BF16)
+    for copy in across + along:
         copy.wait_send()
 
 
@@ -267,7 +350,7 @@
         out_specs=(anywhere, anywhere),
         scratch_shapes=[
             dma((2,)), dma((lines,)), dma((lines,)), dma((lines,)), dma((lines,)),
-            dma((peers,)), dma((peers,)),
+            dma((lines,)), dma((lines,)), dma((peers,)), dma((peers,)),
         ],
         compiler_params=params(0),
     )(hidden.reshape(peers, per, width), meta)
@@ -276,15 +359,15 @@
         cluster_kernel,
         grid_spec=pltpu.PrefetchScalarGridSpec(
             num_scalar_prefetch=1,
-            grid=(peers,),
+            grid=(peers // 2,),
             in_specs=[
-                pl.BlockSpec((peers, 1, per, width), lambda p, t: (0, p, 0, 0)),
-                pl.BlockSpec((1, 8, rows), lambda p, t: (p, 0, 0)),
+                pl.BlockSpec((peers, 2, per, width), lambda p, t: (0, p, 0, 0)),
+                pl.BlockSpec((2, 8, rows), lambda p, t: (p, 0, 0)),
                 pl.BlockSpec((held, BLK, width), lambda p, t: (0, 0, 0)),
             ],
             out_specs=[
-                pl.BlockSpec((peers, 1, per, width), lambda p, t: (0, p, 0, 0)),
-                pl.BlockSpec((1, 8, rows), lambda p, t: (p, 0, 0)),
+                pl.BlockSpec((peers, 2, per, width), lambda p, t: (0, p, 0, 0)),
+                pl.BlockSpec((2, 8, rows), lambda p, t: (p, 0, 0)),
                 pl.BlockSpec((held, BLK, width), lambda p, t: (0, 0, 0)),
             ],
             scratch_shapes=[pltpu.VMEM((held, BLK, width), F32)],
@@ -308,9 +391,10 @@
         scratch_shapes=[
             pltpu.VMEM((lines, peers, per, width), BF16),
             pltpu.VMEM((lines, peers, per, width), BF16),
-            pltpu.VMEM((lines, peers, per, width), BF16),
+            pltpu.VMEM((2, lines, peers, per, width), BF16),
+            pltpu.VMEM((peers, per, width), F32),
             pltpu.VMEM((peers, 8, rows), F32),
-            dma((lines,)), dma((lines,)), dma((lines,)), dma((lines,)),
+            dma((lines,)), dma((lines,)), dma((lines,)), dma((2, lines)),
             dma((peers,)), dma((peers,)),
         ],
         compiler_params=params(1),

time: 194 us -> 167 us (0.86)
  Pallas kernels: 159 us -> 132 us
    pallas_call x1, Pallas kernels: 52 us -> 39.8 us  [local(): pl.pallas_call(functools.partial(scatter_kernel, peers), out_shape=(jax.S...]
    pallas_call x1, Pallas kernels: 51.4 us -> 41.8 us  [local(): pl.pallas_call(functools.partial(gather_kernel, peers), out_shape=(jax.Sh...]
    pallas_call x1, Pallas kernels: 18 us -> 12.8 us  [local(): pl.pallas_call(cluster_kernel, grid_spec=pltpu.PrefetchScalarGridSpec(num...]
where the time goes in v2:
time: 167 us; the launch traced here: 165 us
  Pallas kernels  132 us (79%)
  between operations  14.2 us (9%)
  local copies, waits for them, and re-layouts  9.88 us (6%)
  other arithmetic  5.06 us (3%)
  matrix products  3.97 us (2%)
    pallas_call x1, Pallas kernels, local(): pl.pallas_call(functools.partial(gather_kernel, peers), out_shape=(jax.Sh...  41.8 us
    pallas_call x1, Pallas kernels, local(): pl.pallas_call(functools.partial(scatter_kernel, peers), out_shape=(jax.S...  39.8 us
    pallas_call x1, Pallas kernels, local(): pl.pallas_call(functools.partial(sum_kernel, peers, groups, float(rows *...  37.5 us
    pallas_call x1, Pallas kernels, local(): pl.pallas_call(cluster_kernel, grid_spec=pltpu.PrefetchScalarGridSpec(num...  12.8 us

profile of v2, /device:TPU:0, one launch (start us, length us, event | category | flops | bytes accessed | tf_op | source)
XLA Modules:
  0.0 165.0 jit_solution(14754017846085489442)
XLA Ops:
  7.2 0.0 copy-start
  7.2 0.0 sort.10.cloned.1.call-start
  7.2 1.4 reshape.151
  8.6 0.0 sort.10.cloned.1.call-update
  8.6 0.8 select_reduce_fusion.2
  9.5 0.1 reduce_max.14
  9.5 0.1 reduce_max.18
  9.7 0.1 eq.67
  9.7 0.1 eq.68
  9.8 0.1 reduce_min.14
  9.9 0.1 reduce_min.18
  10.0 0.1 eq.63
  10.1 0.1 eq.64
  10.2 0.9 and_reduce_fusion
  11.1 0.1 reshape.158
  11.2 0.1 broadcast_select_fusion
  11.2 0.1 pad.2.clone
  11.3 0.1 copy.19
  11.4 0.1 reshape.157
  11.5 0.1 copy.18
  11.6 0.1 concatenate.6.table
  11.7 2.0 %sort.10.cloned.1.call-done = s32[8,256]{1,0:T(8,128)} async-done(((s32[8,256]{1,0:T(8,128)}), s32[8,256]{1,0:T(8,128)}) %sort.10.cloned.1.call-update) | async-done | bytes 8208 | tf_op jit(solution)/shard_map/jit(sort)/sort | solution.py:310
  13.7 0.8 dynamic-slice_subtract_fusion
  14.4 0.1 sub.43
  14.5 0.1 sub.46
  14.7 0.9 select_reduce_fusion
  15.6 0.7 constant_dynamic-slice_fusion
  16.3 1.3 convolution_convert_fusion.2
  17.6 0.0 copy-done
  17.6 0.6 add_convert_fusion
  18.2 0.1 add_add_fusion.meta
  18.3 41.8 %shard_map.93 = (bf16[8,8,32,768]{3,2,1,0:T(8,128)(2,1)S(1)}, s32[8,8,256]{2,1,0:T(8,128)S(1)}) custom-call(bf16[8,32,768]{2,1,0:T(8,128)(2,1)S(1)} %bitcast.30, s32[8,256]{1,0:T(8,128)S(1)} %add_add_fusion.meta), custom_call_target="tpu_custom_call" | custom-call | tf_op jit(solution)/shard_map/pallas_call | solution.py:343
  60.1 0.0 copy-start.1
  60.1 1.7 %copy-done.1 = bf16[8,8,32,768]{3,2,1,0:T(8,128)(2,1)} copy-done((bf16[8,8,32,768]{3,2,1,0:T(8,128)(2,1)}, bf16[8,8,32,768]{3,2,1,0:T(8,128)(2,1)S(1)}, u32[]{:S(2)}) %copy-start.1) | copy-done | bytes 3145752
  61.8 12.8 %shard_map.94 = (bf16[8,8,32,768]{3,2,1,0:T(8,128)(2,1)S(1)}, f32[8,8,256]{2,1,0:T(8,128)S(1)}, bf16[20,128,768]{2,1,0:T(8,128)(2,1)}) custom-call(s32[8,7]{1,0:T(8,128)S(1)} %concatenate.6.table, bf16[8,8,32,768]{3,2,1,0:T(8,128)(2,1)} %copy-done.1, s32[8,8,256]{2,1,0:T(8,128)S(1)} %get-tuple-element.12.meta, bf16[20,128,768]{2,1,0:T(8,128)(2,1)} %labels.1), custom_call_target="tpu_custom_call" | custom-call | tf_op jit(solution)/shard_map/pallas_call | solution.py:358
  74.6 39.8 %shard_map.95 = (bf16[8,32,768]{2,1,0:T(8,128)(2,1)S(1)}, f32[8,256]{1,0:T(8,128)S(1)}) custom-call(bf16[8,8,32,768]{3,2,1,0:T(8,128)(2,1)S(1)} %get-tuple-element.13.grads, f32[8,8,256]{2,1,0:T(8,128)S(1)} %get-tuple-element.14.losses), custom_call_target="tpu_custom_call" | custom-call | tf_op jit(solution)/shard_map/pallas_call | solution.py:383
  114.4 0.7 select_reduce_fusion.1
  115.1 0.6 fusion.2
  115.7 0.5 convolution_convert_fusion
  116.2 1.5 convolution_convert_fusion.1
  117.7 0.3 reshape.153
  118.0 0.2 copy.20
  118.2 37.5 %shard_map.96 = bf16[2,2,8,48,384]{4,3,2,1,0:T(8,128)(2,1)S(1)} custom-call(bf16[2,2,8,48,384]{4,3,2,1,0:T(8,128)(2,1)S(1)} %bitcast.28), custom_call_target="tpu_custom_call" | custom-call | tf_op jit(solution)/shard_map/pallas_call | solution.py:413
  155.7 1.2 copy.21
  157.0 1.2 copy.22
  (10 shorter events, 0.1 us)
Async XLA Ops:
  7.2 10.4 %copy-start = (bf16[768,768]{1,0:T(8,128)(2,1)S(1)}, bf16[768,768]{1,0:T(8,128)(2,1)}, u32[]{:S(2)}) copy-start(bf16[768,768]{1,0:T(8,128)(2,1)} %param.8) | copy-start | bytes 3538948
  7.2 6.5 %sort.10.cloned.1.call-start = ((), (), s32[]{:S(2)}) async-start(), calls=%async_computation | async-start | bytes 24608 | tf_op jit(solution)/shard_map/jit(sort)/sort | solution.py:310
  60.1 1.7 %copy-start.1 = (bf16[8,8,32,768]{3,2,1,0:T(8,128)(2,1)}, bf16[8,8,32,768]{3,2,1,0:T(8,128)(2,1)S(1)}, u32[]{:S(2)}) copy-start(bf16[8,8,32,768]{3,2,1,0:T(8,128)(2,1)S(1)} %get-tuple-element.11.hall) | copy-start | bytes 9437188
Sparse Core Ops, SparseCore 0:
  10.9 2.5 sort.12.cloned.1.call-done
  (1 shorter events, 0.0 us)

commit v3 on v2

--- a/solution.py
+++ b/solution.py
@@ -244,47 +244,66 @@
         copy.wait_send()
 
 
-def sum_kernel(peers, groups, scale, term, out, b1, t1, b2, t2, b3, sends, recvs):
+def sum_kernel(peers, groups, scale, term, out, b1, t1, own, b2, t2, b3, sends, recvs):
     me, group = lax.axis_index("dev"), lax.axis_index("grp")
     core, chip, chips = lax.rem(group, 2), group // 2, groups // 2
     partner = {"grp": chip * 2 + 1 - core}
     chip_at = [lax.rem(chip + d, chips) for d in range(chips)]
     dev_at = [lax.rem(me + d, peers) for d in range(peers)]
-    greet(
-        [partner]
-        + [{"grp": chip_at[d] * 2 + core} for d in range(1, chips)]
-        + [{"dev": dev_at[d]} for d in range(1, peers)]
-    )
-    used = [0]
-
-    def make(src, dst, where):
-        at = used[0]
-        used[0] += 1
-        return remote(src, dst, sends.at[at], recvs.at[at], where)
-
-    def run(copies):
-        for copy in copies:
-            copy.start()
-        for copy in copies:
-            copy.wait()
-
-    run([make(term.at[1 - core], b1, partner)])
-    t1[...] = (term[core].astype(F32) + b1[...].astype(F32)).astype(BF16)
-    run([make(t1.at[chip_at[d]], b2.at[d], {"grp": chip_at[d] * 2 + core}) for d in range(1, chips)])
-    acc = t1[chip].astype(F32)
-    for d in range(1, chips):
-        acc = acc + b2[d].astype(F32)
-    t2[...] = acc.astype(BF16)
-    run([make(t2.at[dev_at[d]], b3.at[d], {"dev": dev_at[d]}) for d in range(1, peers)])
-    acc = t2[me].astype(F32)
-    for d in range(1, peers):
-        acc = acc + b3[d].astype(F32)
+    chip_to = [{"grp": at * 2 + core} for at in chip_at]
+    greet([partner] + chip_to[1:] + [{"dev": dev_at[d]} for d in range(1, peers)])
+    far, away = range(1, chips), range(1, peers)
+    pending = []
+
+    def send(src, dst, where):
+        at = len(pending)
+        copy = remote(src, dst, sends.at[at], recvs.at[at], where)
+        copy.start()
+        pending.append(copy)
+        return copy
+
+    halves = [
+        send(term.at[1 - core, chip_at[d]], b1.at[d], partner) for d in list(far) + [0]
+    ]
+    across = {}
+    for d in far:
+        halves[d - 1].wait_recv()
+        t1[d] = (term[core, chip_at[d]].astype(F32) + b1[d].astype(F32)).astype(BF16)
+        for e in list(away) + [0]:
+            across[d, e] = send(t1.at[d, dev_at[e]], b2.at[d, e], chip_to[d])
+    halves[-1].wait_recv()
+    own[...] = term[core, chip].astype(F32) + b1[0].astype(F32)
+    spread = {}
+    for e in list(away) + [0]:
+        acc = own[dev_at[e]]
+        for d in far:
+            across[d, e].wait_recv()
+            acc = acc + b2[d, e].astype(F32)
+        if e > 0:
+            t2[e] = acc.astype(BF16)
+            spread[e] = send(t2.at[e], b3.at[e], {"dev": dev_at[e]})
+    for e in away:
+        spread[e].wait_recv()
+        acc = acc + b3[e].astype(F32)
     out[core, chip, me] = (acc * scale).astype(BF16)
     mine = out.at[core, chip, me]
-    run([make(mine, mine, {"dev": dev_at[d]}) for d in range(1, peers)])
+    back = {e: send(mine, mine, {"dev": dev_at[e]}) for e in away}
+    final = [send(mine, mine, chip_to[d]) for d in far]
+    for e in away:
+        back[e].wait_recv()
+        piece = out.at[core, chip, lax.rem(me + peers - e, peers)]
+        final += [send(piece, piece, chip_to[d]) for d in far]
     mine = out.at[core, chip]
-    run([make(mine, mine, {"grp": chip_at[d] * 2 + core}) for d in range(1, chips)])
-    run([make(out.at[core], out.at[core], partner)])
+    last = [send(mine, mine, partner)]
+    for copy in final:
+        copy.wait_recv()
+    for d in far:
+        mine = out.at[core, chip_at[d]]
+        last.append(send(mine, mine, partner))
+    for copy in last:
+        copy.wait_recv()
+    for copy in pending:
+        copy.wait_send()
 
 
 def params(collective=None):
@@ -409,7 +428,7 @@
     tall, wide = width // (2 * chips * lines), width // 2
     pieces = weight_term.astype(BF16).reshape(2, chips, lines, tall, 2, wide)
     pieces = pieces.transpose(0, 1, 4, 2, 3, 5).reshape(2, chips, peers, tall, wide)
-    count = 2 + 2 * (chips - 1) + 2 * (peers - 1)
+    count = 2 * chips + 2 * (chips - 1) * peers + 2 * (peers - 1)
     summed = pl.pallas_call(
         functools.partial(
             sum_kernel, peers, groups, float(rows * peers * groups) ** (-0.5)
@@ -420,6 +439,7 @@
         scratch_shapes=[
             pltpu.VMEM((chips, peers, tall, wide), BF16),
             pltpu.VMEM((chips, peers, tall, wide), BF16),
+            pltpu.VMEM((peers, tall, wide), F32),
             pltpu.VMEM((chips, peers, tall, wide), BF16),
             pltpu.VMEM((peers, tall, wide), BF16),
             pltpu.VMEM((peers, tall, wide), BF16),

time: 167 us -> 159 us (0.952); the launches traced: 165 us -> 159 us
  Pallas kernels: 132 us -> 126 us
    pallas_call x1, Pallas kernels: 37.5 us -> 31.4 us  [local(): pl.pallas_call(functools.partial(sum_kernel, peers, groups, float(rows *...]
where the time goes in v3:
time: 159 us
  Pallas kernels  126 us (79%)
  between operations  14.2 us (9%)
  local copies, waits for them, and re-layouts  9.88 us (6%)
  other arithmetic  5.06 us (3%)
  matrix products  3.97 us (2%)
    pallas_call x1, Pallas kernels, local(): pl.pallas_call(functools.partial(gather_kernel, peers), out_shape=(jax.Sh...  41.8 us
    pallas_call x1, Pallas kernels, local(): pl.pallas_call(functools.partial(scatter_kernel, peers), out_shape=(jax.S...  39.8 us
    pallas_call x1, Pallas kernels, local(): pl.pallas_call(functools.partial(sum_kernel, peers, groups, float(rows *...  31.4 us
    pallas_call x1, Pallas kernels, local(): pl.pallas_call(cluster_kernel, grid_spec=pltpu.PrefetchScalarGridSpec(num...  12.8 us

profile of v3, /device:TPU:0, one launch (start us, length us, event | category | flops | bytes accessed | tf_op | source)
XLA Modules:
  0.0 158.9 jit_solution(7556854958268280048)
XLA Ops:
  7.2 0.0 copy-start
  7.2 0.0 sort.10.cloned.1.call-start
  7.2 1.4 reshape.151
  8.6 0.0 sort.10.cloned.1.call-update
  8.6 0.8 select_reduce_fusion.2
  9.5 0.1 reduce_max.14
  9.5 0.1 reduce_max.18
  9.7 0.1 eq.67
  9.7 0.1 eq.68
  9.8 0.1 reduce_min.14
  9.9 0.1 reduce_min.18
  10.0 0.1 eq.63
  10.1 0.1 eq.64
  10.2 0.9 and_reduce_fusion
  11.1 0.1 reshape.158
  11.2 0.1 broadcast_select_fusion
  11.2 0.1 pad.2.clone
  11.3 0.1 copy.19
  11.4 0.1 reshape.157
  11.5 0.1 copy.18
  11.6 0.1 concatenate.6.table
  11.7 2.0 %sort.10.cloned.1.call-done = s32[8,256]{1,0:T(8,128)} async-done(((s32[8,256]{1,0:T(8,128)}), s32[8,256]{1,0:T(8,128)}) %sort.10.cloned.1.call-update) | async-done | bytes 8208 | tf_op jit(solution)/shard_map/jit(sort)/sort | solution.py:329
  13.7 0.8 dynamic-slice_subtract_fusion
  14.4 0.1 sub.43
  14.5 0.1 sub.46
  14.7 0.9 select_reduce_fusion
  15.6 0.7 constant_dynamic-slice_fusion
  16.3 1.3 convolution_convert_fusion.2
  17.6 0.0 copy-done
  17.6 0.6 add_convert_fusion
  18.2 0.1 add_add_fusion.meta
  18.3 41.8 %shard_map.93 = (bf16[8,8,32,768]{3,2,1,0:T(8,128)(2,1)S(1)}, s32[8,8,256]{2,1,0:T(8,128)S(1)}) custom-call(bf16[8,32,768]{2,1,0:T(8,128)(2,1)S(1)} %bitcast.30, s32[8,256]{1,0:T(8,128)S(1)} %add_add_fusion.meta), custom_call_target="tpu_custom_call" | custom-call | tf_op jit(solution)/shard_map/pallas_call | solution.py:362
  60.1 0.0 copy-start.1
  60.1 1.7 %copy-done.1 = bf16[8,8,32,768]{3,2,1,0:T(8,128)(2,1)} copy-done((bf16[8,8,32,768]{3,2,1,0:T(8,128)(2,1)}, bf16[8,8,32,768]{3,2,1,0:T(8,128)(2,1)S(1)}, u32[]{:S(2)}) %copy-start.1) | copy-done | bytes 3145752
  61.8 12.8 %shard_map.94 = (bf16[8,8,32,768]{3,2,1,0:T(8,128)(2,1)S(1)}, f32[8,8,256]{2,1,0:T(8,128)S(1)}, bf16[20,128,768]{2,1,0:T(8,128)(2,1)}) custom-call(s32[8,7]{1,0:T(8,128)S(1)} %concatenate.6.table, bf16[8,8,32,768]{3,2,1,0:T(8,128)(2,1)} %copy-done.1, s32[8,8,256]{2,1,0:T(8,128)S(1)} %get-tuple-element.12.meta, bf16[20,128,768]{2,1,0:T(8,128)(2,1)} %labels.1), custom_call_target="tpu_custom_call" | custom-call | tf_op jit(solution)/shard_map/pallas_call | solution.py:377
  74.6 39.8 %shard_map.95 = (bf16[8,32,768]{2,1,0:T(8,128)(2,1)S(1)}, f32[8,256]{1,0:T(8,128)S(1)}) custom-call(bf16[8,8,32,768]{3,2,1,0:T(8,128)(2,1)S(1)} %get-tuple-element.13.grads, f32[8,8,256]{2,1,0:T(8,128)S(1)} %get-tuple-element.14.losses), custom_call_target="tpu_custom_call" | custom-call | tf_op jit(solution)/shard_map/pallas_call | solution.py:402
  114.4 0.7 select_reduce_fusion.1
  115.1 0.6 fusion.2
  115.7 0.5 convolution_convert_fusion
  116.2 1.5 convolution_convert_fusion.1
  117.7 0.3 reshape.153
  118.0 0.2 copy.20
  118.2 31.4 %shard_map.96 = bf16[2,2,8,48,384]{4,3,2,1,0:T(8,128)(2,1)S(1)} custom-call(bf16[2,2,8,48,384]{4,3,2,1,0:T(8,128)(2,1)S(1)} %bitcast.28), custom_call_target="tpu_custom_call" | custom-call | tf_op jit(solution)/shard_map/pallas_call | solution.py:432
  149.6 1.2 copy.21
  150.8 1.2 copy.22
  (10 shorter events, 0.1 us)
Async XLA Ops:
  7.2 10.4 %copy-start = (bf16[768,768]{1,0:T(8,128)(2,1)S(1)}, bf16[768,768]{1,0:T(8,128)(2,1)}, u32[]{:S(2)}) copy-start(bf16[768,768]{1,0:T(8,128)(2,1)} %param.8) | copy-start | bytes 3538948
  7.2 6.5 %sort.10.cloned.1.call-start = ((), (), s32[]{:S(2)}) async-start(), calls=%async_computation | async-start | bytes 24608 | tf_op jit(solution)/shard_map/jit(sort)/sort | solution.py:329
  60.1 1.7 %copy-start.1 = (bf16[8,8,32,768]{3,2,1,0:T(8,128)(2,1)}, bf16[8,8,32,768]{3,2,1,0:T(8,128)(2,1)S(1)}, u32[]{:S(2)}) copy-start(bf16[8,8,32,768]{3,2,1,0:T(8,128)(2,1)S(1)} %get-tuple-element.11.hall) | copy-start | bytes 9437188
Sparse Core Ops, SparseCore 0:
  10.9 2.5 sort.12.cloned.1.call-done
  (1 shorter events, 0.0 us)

commit v4 on v3

--- a/solution.py
+++ b/solution.py
@@ -306,9 +306,9 @@
         copy.wait_send()
 
 
-def params(collective=None):
+def params(collective=None, limit=48):
     more = {} if collective is None else dict(collective_id=collective, has_side_effects=True)
-    return pltpu.CompilerParams(vmem_limit_bytes=48 * 1024 * 1024, **more)
+    return pltpu.CompilerParams(vmem_limit_bytes=limit * 1024 * 1024, **more)
 
 
 def local(queries, query_slots, w_res, labels, blocks, positives):
@@ -371,7 +371,7 @@
             dma((2,)), dma((lines,)), dma((lines,)), dma((lines,)), dma((lines,)),
             dma((lines,)), dma((lines,)), dma((peers,)), dma((peers,)),
         ],
-        compiler_params=params(0),
+        compiler_params=params(0, 62),
     )(hidden.reshape(peers, per, width), meta)
 
     grads, losses, label_grad = pl.pallas_call(
@@ -396,7 +396,7 @@
             jax.ShapeDtypeStruct((peers, 8, rows), F32),
             jax.ShapeDtypeStruct(labels.shape, BF16),
         ),
-        compiler_params=params(),
+        compiler_params=params(limit=62),
     )(table, hall, mall, labels)
 
     hidden_grad, loss_sum = pl.pallas_call(

time: 159 us -> 164 us (1.031)
  Pallas kernels: 126 us -> 128 us
    pallas_call x1, Pallas kernels: 39.8 us -> 41.6 us  [local(): pl.pallas_call(functools.partial(scatter_kernel, peers), out_shape=(jax.S...]
    unnamed x6 -> x12, local copies, waits for them, and re-layouts: 2.93 us -> 4.01 us
where the time goes in v4:
time: 164 us; the launch traced here: 163 us
  Pallas kernels  128 us (78%)
  between operations  14.2 us (9%)
  local copies, waits for them, and re-layouts  11 us (7%)
  other arithmetic  5.65 us (3%)
  matrix products  4.72 us (3%)
    pallas_call x1, Pallas kernels, local(): pl.pallas_call(functools.partial(gather_kernel, peers), out_shape=(jax.Sh...  42.5 us
    pallas_call x1, Pallas kernels, local(): pl.pallas_call(functools.partial(scatter_kernel, peers), out_shape=(jax.S...  41.6 us
    pallas_call x1, Pallas kernels, local(): pl.pallas_call(functools.partial(sum_kernel, peers, groups, float(rows *...  30.4 us
    pallas_call x1, Pallas kernels, local(): pl.pallas_call(cluster_kernel, grid_spec=pltpu.PrefetchScalarGridSpec(num...  13.1 us
    unnamed x12, local copies, waits for them, and re-layouts  4.01 us

profile of v4, /device:TPU:0, one launch (start us, length us, event | category | flops | bytes accessed | tf_op | source)
XLA Modules:
  0.0 163.1 jit_solution(922088306122069835)
XLA Ops:
  7.2 0.0 copy-start
  7.2 0.0 sort.10.cloned.1.call-start
  7.2 1.4 reshape.151
  8.6 0.0 sort.10.cloned.1.call-update
  8.6 0.8 select_reduce_fusion.2
  9.5 0.1 reduce_max.14
  9.5 0.1 reduce_max.18
  9.7 0.1 eq.67
  9.7 0.1 eq.68
  9.8 0.1 reduce_min.14
  9.9 0.1 reduce_min.18
  10.0 0.1 eq.63
  10.1 0.1 eq.64
  10.2 0.9 and_reduce_fusion
  11.1 0.1 reshape.158
  11.2 0.1 broadcast_select_fusion
  11.2 0.1 pad.2.clone
  11.3 0.1 copy.19
  11.4 0.1 reshape.157
  11.5 0.1 copy.18
  11.6 0.7 concatenate.6.table
  12.3 1.4 sort.10.cloned.1.call-done
  13.7 0.8 dynamic-slice_subtract_fusion
  14.4 0.1 sub.43
  14.5 0.1 sub.46
  14.7 0.9 select_reduce_fusion
  15.6 0.7 constant_dynamic-slice_fusion
  16.3 1.3 convolution_convert_fusion.2
  17.6 0.0 copy-done
  17.6 0.0 copy-start.3
  17.6 1.4 add_convert_fusion
  19.0 0.0 copy-done.3
  19.0 0.7 add_add_fusion.meta
  19.7 42.5 %shard_map.93 = (bf16[8,8,32,768]{3,2,1,0:T(8,128)(2,1)}, s32[8,8,256]{2,1,0:T(8,128)}) custom-call(bf16[8,32,768]{2,1,0:T(8,128)(2,1)} %bitcast.33, s32[8,256]{1,0:T(8,128)} %add_add_fusion.meta), custom_call_target="tpu_custom_call" | custom-call | tf_op jit(solution)/shard_map/pallas_call | solution.py:362
  62.2 13.1 %shard_map.94 = (bf16[8,8,32,768]{3,2,1,0:T(8,128)(2,1)}, f32[8,8,256]{2,1,0:T(8,128)}, bf16[20,128,768]{2,1,0:T(8,128)(2,1)}) custom-call(s32[8,7]{1,0:T(8,128)} %concatenate.6.table, bf16[8,8,32,768]{3,2,1,0:T(8,128)(2,1)} %get-tuple-element.11.hall, s32[8,8,256]{2,1,0:T(8,128)} %get-tuple-element.12.meta, bf16[20,128,768]{2,1,0:T(8,128)(2,1)} %labels.1), custom_call_target="tpu_custom_call" | custom-call | tf_op jit(solution)/shard_map/pallas_call | solution.py:377
  75.2 1.9 %copy-done.1 = bf16[8,8,32,768]{3,2,1,0:T(8,128)(2,1)S(1)} copy-done((bf16[8,8,32,768]{3,2,1,0:T(8,128)(2,1)S(1)}, bf16[8,8,32,768]{3,2,1,0:T(8,128)(2,1)}, u32[]{:S(2)}) %copy-start.1) | copy-done | bytes 3145752
  77.1 0.8 copy-done.2
  78.0 41.6 %shard_map.95 = (bf16[8,32,768]{2,1,0:T(8,128)(2,1)S(1)}, f32[8,256]{1,0:T(8,128)S(1)}) custom-call(bf16[8,8,32,768]{3,2,1,0:T(8,128)(2,1)S(1)} %copy-done.1, f32[8,8,256]{2,1,0:T(8,128)S(1)} %copy-done.2), custom_call_target="tpu_custom_call" | custom-call | tf_op jit(solution)/shard_map/pallas_call | solution.py:402
  119.6 0.0 copy-start.4
  119.6 0.7 select_reduce_fusion.1
  120.3 0.6 fusion.2
  120.8 0.5 convolution_convert_fusion
  121.3 1.5 convolution_convert_fusion.1
  122.9 0.3 reshape.153
  123.2 0.2 copy.20
  123.4 30.4 %shard_map.96 = bf16[2,2,8,48,384]{4,3,2,1,0:T(8,128)(2,1)S(1)} custom-call(bf16[2,2,8,48,384]{4,3,2,1,0:T(8,128)(2,1)S(1)} %bitcast.28), custom_call_target="tpu_custom_call" | custom-call | tf_op jit(solution)/shard_map/pallas_call | solution.py:432
  153.8 1.2 copy.21
  155.0 1.2 copy.22
  (13 shorter events, 0.1 us)
Async XLA Ops:
  7.2 10.4 %copy-start = (bf16[768,768]{1,0:T(8,128)(2,1)S(1)}, bf16[768,768]{1,0:T(8,128)(2,1)}, u32[]{:S(2)}) copy-start(bf16[768,768]{1,0:T(8,128)(2,1)} %param.8) | copy-start | bytes 3538948
  7.2 6.5 %sort.10.cloned.1.call-start = ((), (), s32[]{:S(2)}) async-start(), calls=%async_computation | async-start | bytes 24608 | tf_op jit(solution)/shard_map/jit(sort)/sort | solution.py:329
  17.6 1.4 copy-start.3
  75.2 1.9 %copy-start.1 = (bf16[8,8,32,768]{3,2,1,0:T(8,128)(2,1)S(1)}, bf16[8,8,32,768]{3,2,1,0:T(8,128)(2,1)}, u32[]{:S(2)}) copy-start(bf16[8,8,32,768]{3,2,1,0:T(8,128)(2,1)} %get-tuple-element.13.grads) | copy-start | bytes 9437188
  77.1 0.8 copy-start.2
  119.6 1.3 copy-start.4
Sparse Core Ops, SparseCore 0:
  10.9 2.5 sort.12.cloned.1.call-done
  (1 shorter events, 0.0 us)
